TPU v7x, 32 devices: a whole 2x2x4 slice. The times are simulated.
32 devices in a mesh: prow: 8 (over z, x), pcol: 4 (over y, core).
Axes of the slice: x: 2, y: 2, z: 4, core: 2. Of those that a mesh axis runs over, the one named last changes fastest.
Arguments:
- right_side: float32 [512, 8192], P('pcol', 'prow'), may hold values from -6 to 6
- factor: float32 [8192, 2048], P('prow', 'pcol'), may hold values from -0.125 to 0.125
- inverses: float32 [2048, 512], replicated, as said below
Outputs:
- solved: float32 [512, 8192], P('pcol', 'prow')
Inputs may be any that keep to these rules, and one draw needn't show every extreme that they name: Each 512 x 512 block of inverses is lower triangular with a positive diagonal.
All inputs are finite; a program needn't handle non-finite values.
Results may differ from a plain program's by a relative error of at most 0.0001.
Values sent between devices are 32-bit elements; how exact they have to be, the bound alone decides.
A program may use at most 64 MiB of HBM per device.

v0:
```python
import jax
import jax.numpy as jnp
from jax import lax
from jax.sharding import PartitionSpec as P


def spread(block, axis, source):
    block = jnp.where(lax.axis_index(axis) == source, block, jnp.zeros_like(block))
    return lax.psum(block, axis)


def contract(left, right):
    return lax.dot_general(
        left,
        right,
        (((1,), (1,)), ((), ())),
        precision=lax.Precision.HIGHEST,
        preferred_element_type=jnp.float32,
    )


def per_device(right_side, factor, inverses):
    block = factor.shape[1]
    rhs_width = right_side.shape[0]
    sections = lax.axis_size("pcol")
    all_samples = rhs_width * sections
    row_at = lax.axis_index("prow")
    col_at = lax.axis_index("pcol")
    top_block = factor[:block]
    panel_own = jnp.zeros((all_samples, block), jnp.float32)
    solved_head = jnp.zeros((rhs_width, block), jnp.float32)
    own_panels = []
    for section in range(sections):
        current = right_side[:, :block]
        if section > 0:
            current = current - lax.psum_scatter(
                contract(panel_own, top_block), "pcol", scatter_dimension=0, tiled=True
            )
        block_inverse = inverses[section * block : (section + 1) * block]
        solved_part = contract(current, block_inverse)
        solved_head = jnp.where(row_at == section, solved_part, solved_head)
        gathered = lax.all_gather(solved_part, "pcol", axis=0, tiled=True)
        panel_full = spread(gathered, "prow", section)
        panel_own = jnp.where(col_at == section, panel_full, panel_own)
        own_panels.append(lax.dynamic_slice_in_dim(panel_full, col_at * rhs_width, rhs_width, 0))
    updated = right_side - lax.psum_scatter(
        contract(panel_own, factor), "pcol", scatter_dimension=0, tiled=True
    )
    head_block = jnp.where(row_at < sections, solved_head, updated[:, :block])
    return jnp.concatenate([head_block, updated[:, block:]], axis=1)


def solution(mesh):
    return jax.shard_map(
        per_device,
        mesh=mesh,
        in_specs=(P("pcol", "prow"), P("prow", "pcol"), P()),
        out_specs=P("pcol", "prow"),
        check_vma=False,
    )
```

profile of v0, /device:TPU:29, one launch (start us, length us, event | category | flops | bytes accessed | tf_op | source)
XLA Modules:
  0.0 544.7 jit_solution(904137054482911266)
XLA Ops:
  6.5 3.2 fusion.8
  9.7 0.0 all-reduce.5.cloned.1.call-start
  9.8 17.2 %all-gather.5.cloned.1.call-done = f32[512,512]{1,0:T(8,128)} async-done(((f32[128,512]{1,0:T(8,128)}), f32[512,512]{1,0:T(8,128)}) %all-gather.5.cloned.1.call-update) | async-done | bytes 1048592 | tf_op jit(solution)/shard_map/all_gather | solution.py:42
  27.0 1.1 broadcast_select_fusion.3
  28.2 78.6 %all-reduce.5.cloned.1.call-done = f32[512,512]{1,0:T(8,128)} async-done(((f32[512,512]{1,0:T(8,128)}), f32[512,512]{1,0:T(8,128)}) %all-reduce.5.cloned.1.call-update) | async-done | bytes 1048592 | tf_op jit(solution)/shard_map/psum | solution.py:9
  106.8 2.8 fusion.10
  109.7 26.5 %reduce-scatter.5.cloned.1.call-done = f32[128,512]{1,0:T(8,128)} async-done(((f32[512,512]{1,0:T(8,128)}), f32[128,512]{1,0:T(8,128)}) %reduce-scatter.5.cloned.1.call-update) | async-done | bytes 262160 | tf_op jit(solution)/shard_map/reduce_scatter | solution.py:36
  136.2 3.2 fusion.6
  139.4 17.2 %all-gather.7.cloned.1.call-done = f32[512,512]{1,0:T(8,128)} async-done(((f32[128,512]{1,0:T(8,128)}), f32[512,512]{1,0:T(8,128)}) %all-gather.7.cloned.1.call-update) | async-done | bytes 1048592 | tf_op jit(solution)/shard_map/all_gather | solution.py:42
  156.7 1.1 broadcast_select_fusion.2
  157.8 78.5 %all-reduce.7.cloned.1.call-done = f32[512,512]{1,0:T(8,128)} async-done(((f32[512,512]{1,0:T(8,128)}), f32[512,512]{1,0:T(8,128)}) %all-reduce.7.cloned.1.call-update) | async-done | bytes 1048592 | tf_op jit(solution)/shard_map/psum | solution.py:9
  236.3 0.2 select_select_fusion
  236.5 2.8 fusion.14
  239.4 26.5 %reduce-scatter.7.cloned.1.call-done = f32[128,512]{1,0:T(8,128)} async-done(((f32[512,512]{1,0:T(8,128)}), f32[128,512]{1,0:T(8,128)}) %reduce-scatter.7.cloned.1.call-update) | async-done | bytes 262160 | tf_op jit(solution)/shard_map/reduce_scatter | solution.py:36
  265.9 3.3 fusion.4
  269.2 17.2 %all-gather.9.cloned.1.call-done = f32[512,512]{1,0:T(8,128)} async-done(((f32[128,512]{1,0:T(8,128)}), f32[512,512]{1,0:T(8,128)}) %all-gather.9.cloned.1.call-update) | async-done | bytes 1048592 | tf_op jit(solution)/shard_map/all_gather | solution.py:42
  286.5 1.1 broadcast_select_fusion.1
  287.6 78.6 %all-reduce.9.cloned.1.call-done = f32[512,512]{1,0:T(8,128)} async-done(((f32[512,512]{1,0:T(8,128)}), f32[512,512]{1,0:T(8,128)}) %all-reduce.9.cloned.1.call-update) | async-done | bytes 1048592 | tf_op jit(solution)/shard_map/psum | solution.py:9
  366.2 2.8 fusion.12
  369.1 0.0 all-gather.11.cloned.1.call-start
  369.1 27.4 %reduce-scatter.9.cloned.1.call-done = f32[128,512]{1,0:T(8,128)} async-done(((f32[512,512]{1,0:T(8,128)}), f32[128,512]{1,0:T(8,128)}) %reduce-scatter.9.cloned.1.call-update) | async-done | bytes 262160 | tf_op jit(solution)/shard_map/reduce_scatter | solution.py:36
  396.5 3.3 fusion.2
  399.8 0.0 all-reduce.11.cloned.1.call-start
  399.9 17.2 %all-gather.11.cloned.1.call-done = f32[512,512]{1,0:T(8,128)} async-done(((f32[128,512]{1,0:T(8,128)}), f32[512,512]{1,0:T(8,128)}) %all-gather.11.cloned.1.call-update) | async-done | bytes 1048592 | tf_op jit(solution)/shard_map/all_gather | solution.py:42
  417.1 1.1 broadcast_select_fusion
  418.2 0.2 reduce-scatter.11.cloned.1.call-start
  418.4 78.4 %all-reduce.11.cloned.1.call-done = f32[512,512]{1,0:T(8,128)} async-done(((f32[512,512]{1,0:T(8,128)}), f32[512,512]{1,0:T(8,128)}) %all-reduce.11.cloned.1.call-update) | async-done | bytes 1048592 | tf_op jit(solution)/shard_map/psum | solution.py:9
  496.8 6.1 %fusion = f32[512,1024]{1,0:T(8,128)} fusion(f32[1024,512]{1,0:T(8,128)S(1)} %copy-done, f32[512,512]{1,0:T(8,128)} %all-reduce.11.cloned.1.call-done, pred[]{:T(512)S(6)} %eq.35, f32[512,512]{1,0:T(8,128)} %all-reduce.9.cloned.1.call-done, f32[512,512]{1,0:T(8,128)S(1)} %select_select_fusion, pred[]{:T(512)S(6)} %eq.29), kind=kOutput, calls=%fused_computation | convolution fusion | flops 3221749760 | bytes 7340034 | tf_op jit(solution)/shard_map/dot_general | solution.py:13
  503.0 32.7 %reduce-scatter.11.cloned.1.call-done = f32[128,1024]{1,0:T(8,128)} async-done(((f32[512,1024]{1,0:T(8,128)}), f32[128,1024]{1,0:T(8,128)}) %reduce-scatter.11.cloned.1.call-update) | async-done | bytes 524304 | tf_op jit(solution)/shard_map/reduce_scatter | solution.py:46
  535.7 1.1 sub.15
  536.9 0.2 slice_select_fusion
  537.1 0.8 copy-done.7
  (36 shorter events, 0.5 us)
Async XLA Ops:
  6.5 20.5 %all-gather.5.cloned.1.call-start = ((), (), s32[]{:S(2)}) async-start(), calls=%async_computation.4 | async-start | bytes 1310720 | tf_op jit(solution)/shard_map/all_gather | solution.py:42
  9.7 97.1 %copy-start = (f32[1024,512]{1,0:T(8,128)S(1)}, f32[1024,512]{1,0:T(8,128)}, u32[]{:S(2)}) copy-start(f32[1024,512]{1,0:T(8,128)} %param.4) | copy-start | bytes 6291460
  9.7 97.0 %all-reduce.5.cloned.1.call-start = ((), (), s32[]{:S(2)}) async-start(), calls=%async_computation.5 | async-start | bytes 2097152 | tf_op jit(solution)/shard_map/psum | solution.py:9
  28.1 108.0 %reduce-scatter.5.cloned.1.call-start = ((), (), s32[]{:S(2)}) async-start(), calls=%async_computation.6 | async-start | bytes 1310720 | tf_op jit(solution)/shard_map/reduce_scatter | solution.py:36
  28.2 108.0 %copy-start.1 = (f32[128,1024]{1,0:T(8,128)S(1)}, f32[128,1024]{1,0:T(8,128)}, u32[]{:S(2)}) copy-start(f32[128,1024]{1,0:T(8,128)} %param.3) | copy-start | bytes 1572868
  109.6 47.0 %all-gather.7.cloned.1.call-start = ((), (), s32[]{:S(2)}) async-start(), calls=%async_computation.7 | async-start | bytes 1310720 | tf_op jit(solution)/shard_map/all_gather | solution.py:42
  139.4 96.9 %all-reduce.7.cloned.1.call-start = ((), (), s32[]{:S(2)}) async-start(), calls=%async_computation.8 | async-start | bytes 2097152 | tf_op jit(solution)/shard_map/psum | solution.py:9
  157.7 108.1 %reduce-scatter.7.cloned.1.call-start = ((), (), s32[]{:S(2)}) async-start(), calls=%async_computation.9 | async-start | bytes 1310720 | tf_op jit(solution)/shard_map/reduce_scatter | solution.py:36
  239.4 47.1 %all-gather.9.cloned.1.call-start = ((), (), s32[]{:S(2)}) async-start(), calls=%async_computation.10 | async-start | bytes 1310720 | tf_op jit(solution)/shard_map/all_gather | solution.py:42
  269.2 97.0 %all-reduce.9.cloned.1.call-start = ((), (), s32[]{:S(2)}) async-start(), calls=%async_computation.11 | async-start | bytes 2097152 | tf_op jit(solution)/shard_map/psum | solution.py:9
  287.6 108.9 %reduce-scatter.9.cloned.1.call-start = ((), (), s32[]{:S(2)}) async-start(), calls=%async_computation.12 | async-start | bytes 1310720 | tf_op jit(solution)/shard_map/reduce_scatter | solution.py:36
  369.1 48.0 %all-gather.11.cloned.1.call-start = ((), (), s32[]{:S(2)}) async-start(), calls=%async_computation.13 | async-start | bytes 1310720 | tf_op jit(solution)/shard_map/all_gather | solution.py:42
  399.8 97.0 %all-reduce.11.cloned.1.call-start = ((), (), s32[]{:S(2)}) async-start(), calls=%async_computation.14 | async-start | bytes 2097152 | tf_op jit(solution)/shard_map/psum | solution.py:9
  418.2 117.6 %reduce-scatter.11.cloned.1.call-start = ((), (), s32[]{:S(2)}) async-start(), calls=%async_computation.15 | async-start | bytes 2621440 | tf_op jit(solution)/shard_map/reduce_scatter | solution.py:46
  503.0 32.8 %copy-start.2 = (f32[128,1024]{1,0:T(8,128)S(1)}, f32[128,1024]{1,0:T(8,128)}, u32[]{:S(2)}) copy-start(f32[128,1024]{1,0:T(8,128)} %param.3) | copy-start | bytes 1572868
  503.0 33.9 %copy-start.3 = (f32[128,512]{1,0:T(8,128)S(1)}, f32[128,512]{1,0:T(8,128)}, u32[]{:S(2)}) copy-start(f32[128,512]{1,0:T(8,128)} %fusion.6) | copy-start | bytes 786436
  503.0 33.9 %copy-start.4 = (f32[128,512]{1,0:T(8,128)S(1)}, f32[128,512]{1,0:T(8,128)}, u32[]{:S(2)}) copy-start(f32[128,512]{1,0:T(8,128)} %fusion.4) | copy-start | bytes 786436
  503.0 33.9 %copy-start.5 = (f32[128,512]{1,0:T(8,128)S(1)}, f32[128,512]{1,0:T(8,128)}, u32[]{:S(2)}) copy-start(f32[128,512]{1,0:T(8,128)} %fusion.2) | copy-start | bytes 786436
  503.0 33.9 %copy-start.6 = (f32[128,512]{1,0:T(8,128)S(1)}, f32[128,512]{1,0:T(8,128)}, u32[]{:S(2)}) copy-start(f32[128,512]{1,0:T(8,128)} %fusion.8) | copy-start | bytes 786436
  537.1 0.8 copy-start.7
Sparse Core Ops, SparseCore 0:
  9.9 17.1 all-gather.4
  30.5 76.1 all-reduce.4
  109.8 26.3 reduce-scatter.4
  139.5 17.1 all-gather.6
  160.0 76.2 all-reduce.6
  239.5 26.3 reduce-scatter.6
  269.3 17.1 all-gather.8
  290.0 76.2 all-reduce.8
  369.2 27.2 reduce-scatter.8
  399.9 17.0 all-gather.10
  420.6 76.2 all-reduce.10
  503.1 32.5 reduce-scatter.10
where the time goes:
time: 548 us; the launch traced here: 545 us
  waiting for transfers between devices  496 us (91%)
  matrix products  27.6 us (5%)
  between operations  13.7 us (2%)
  other arithmetic  5.78 us (1%)
    psum x4, waiting for transfers between devices, spread(): return lax.psum(block, axis)  314 us
    reduce_scatter x3, waiting for transfers between devices, per_device(): lax.psum_scatter(contract(panel_own, top_block), 'pcol', scatter_dimensio...  80.3 us
    all_gather x4, waiting for transfers between devices, per_device(): gathered = lax.all_gather(solved_part, 'pcol', axis=0, tiled=True)  68.9 us
    reduce_scatter x1, waiting for transfers between devices, per_device(): lax.psum_scatter(contract(panel_own, factor), 'pcol', scatter_dimension=0...  32.7 us
    dot_general x8, matrix products, contract(): lax.dot_general(left, right, (((1,), (1,)), ((), ())), precision=lax.Prec...  27.6 us
  transfers between devices with their start and end apart: 12, of which 12 were waited for; matrix products, arithmetic and copies ran while one was open for 0% of the time, Pallas kernels for 0%

commit v1 on v0

v1 whole, which is shorter than its diff:
```python
import functools

import jax
import jax.numpy as jnp
from jax import lax
from jax.experimental import pallas as pl
from jax.experimental.pallas import tpu as pltpu
from jax.sharding import PartitionSpec as P

MESH = pl.DeviceIdType.MESH
SUBS = 2
HALVES = 2


def split(value):
    high = value.astype(jnp.bfloat16)
    low = (value - high.astype(jnp.float32)).astype(jnp.bfloat16)
    return high, low


def dot_nt(left, right):
    return lax.dot_general(left, right, (((1,), (1,)), ((), ())), preferred_element_type=jnp.float32)


def contract(left, right_high, right_low):
    rows = left.shape[0]
    high, low = split(left)
    both = dot_nt(jnp.concatenate([high, low], axis=0), right_high)
    return both[:rows] + (both[rows:] + dot_nt(high, right_low))


def kernel(
    n_prow, sections, rhs, factor, inverses, out,
    fac, fac_hi, fac_lo, dinv, d_hi, d_lo, l_in, l_hi, l_lo,
    acc, x_own, x_head, x_all, part, pre, fin, cross,
    local_sem, l_send, l_fwd, l_recv, head_send, head_recv, gather_send,
    tree_send, x_recv, part_send, pre_recv, fin_recv, cross_recv,
):
    width = rhs.shape[0]
    block = factor.shape[1]
    blocks = factor.shape[0] // block
    p = lax.axis_index("prow")
    c = lax.axis_index("pcol")
    pair, parity = c // 2, c % 2
    mate = pair * 2 + 1 - parity
    over = (1 - pair) * 2 + parity
    far = (1 - pair) * 2 + 1 - parity
    in_head = p < sections
    sub = width // SUBS
    half = block // HALVES

    fac_copy = pltpu.make_async_copy(factor, fac, local_sem.at[0])
    fac_copy.start()
    dinv_copy = pltpu.make_async_copy(
        inverses.at[pl.ds(lax.rem(p, sections) * block, block)], dinv, local_sem.at[1]
    )
    dinv_copy.start()

    barrier = pltpu.get_barrier_semaphore()
    for step in range(1, n_prow):
        pl.semaphore_signal(
            barrier, inc=1, device_id=(lax.rem(p + step, n_prow), c), device_id_type=MESH
        )
    for step in range(1, sections):
        pl.semaphore_signal(
            barrier, inc=1, device_id=(p, lax.rem(c + step, sections)), device_id_type=MESH
        )
    pl.semaphore_wait(barrier, n_prow - 1 + sections - 1)

    def send(src, dst, send_sem, recv_sem, row, col):
        return pltpu.make_async_remote_copy(
            src_ref=src, dst_ref=dst, send_sem=send_sem, recv_sem=recv_sem,
            device_id=(row, col), device_id_type=MESH,
        )

    def l_piece(j, h):
        return l_in.at[j, pl.ds(h * half, half)]

    def l_copy(j, h, target, way):
        return send(
            factor.at[pl.ds(h * half, half)], l_piece(j, h), l_send.at[way, h], l_recv.at[j, h], p, target
        )

    def l_forward(j, h):
        return send(l_piece(j, h), l_piece(j, h), l_fwd.at[j, h], l_recv.at[j, h], p, j ^ 3)

    for j in range(sections - 1):
        @pl.when((p > j) & in_head & (c == j))
        def _():
            for h in range(HALVES):
                l_copy(j, h, j ^ 2, 0).start()
                l_copy(j, h, j ^ 1, 1).start()

    dinv_copy.wait()
    d_hi[...], d_lo[...] = split(dinv[...])
    fac_copy.wait()
    fac_hi[...], fac_lo[...] = split(fac[...])

    for j in range(sections - 1):
        @pl.when((p > j) & in_head & (c == j))
        def _():
            l_hi[j], l_lo[j] = fac_hi[:block], fac_lo[:block]

        @pl.when((p > j) & in_head & (c == (j ^ 2)))
        def _():
            for h in range(HALVES):
                l_forward(j, h).wait_recv()
                l_forward(j, h).start()
            l_hi[j], l_lo[j] = split(l_in[j])

    for j in range(sections - 1):
        @pl.when((p > j) & in_head & ((c == (j ^ 1)) | (c == (j ^ 3))))
        def _():
            for h in range(HALVES):
                l_forward(j, h).wait_recv()
            l_hi[j], l_lo[j] = split(l_in[j])

    def head_copy(s, target, col):
        rows = pl.ds(s * sub, sub)
        return send(
            x_own.at[rows], x_head.at[col, rows], head_send.at[target, s], head_recv.at[col, s], target, c
        )

    def gather_copy(s):
        rows = pl.ds(s * sub, sub)
        return send(x_own.at[rows], x_all.at[c, rows], gather_send.at[s], x_recv.at[c, s], p, p)

    @pl.when(in_head)
    def _():
        for s in range(SUBS):
            rows = pl.ds(s * sub, sub)
            acc[...] = rhs[rows, :block]
            for j in range(sections - 1):
                @pl.when(j < p)
                def _():
                    head_copy(s, sections - 1, j).wait_recv()
                    acc[...] -= contract(x_head[j, rows], l_hi[j], l_lo[j])
            x_own[rows] = contract(acc[...], d_hi[...], d_lo[...])
            for target in range(1, sections):
                @pl.when(p < target)
                def _():
                    head_copy(s, target, p).start()

            @pl.when(p != c)
            def _():
                gather_copy(s).start()

            @pl.when(p == c)
            def _():
                x_all[c, rows] = x_own[rows]

    z, x = p // 2, p % 2
    root_z, root_x = c // 2, c % 2
    links = (
        ((x == root_x) & (z >= root_z) & (z + 1 < n_prow // 2), p + 2),
        ((x == root_x) & (z <= root_z) & (z > 0), p - 2),
        (x == root_x, z * 2 + 1 - x),
    )

    def tree_copy(q, s, way, target):
        ref = x_all.at[q, pl.ds(s * sub, sub)]
        return send(ref, ref, tree_send.at[way, q, s], x_recv.at[q, s], target, c)

    def part_copy(i, r):
        if i == 0:
            return send(part.at[i, r], pre.at[r], part_send.at[i, r], pre_recv.at[r], p, mate)
        if i == 1:
            return send(part.at[i, r], cross.at[r], part_send.at[i, r], cross_recv.at[r], p, over)
        return send(part.at[i, r], fin.at[r], part_send.at[i, r], fin_recv.at[r], p, mate)

    def each_block(body):
        for r in range(blocks):
            if r == 0:
                pl.when(p >= sections)(functools.partial(body, r))
            else:
                body(r)

    order = (far, over, mate, c)
    for i, q in enumerate(order):
        for s in range(SUBS):
            @pl.when((p != c) | (q != c))
            def _():
                tree_copy(q, s, 2, mate).wait_recv()

            for way, (active, target) in enumerate(links):
                @pl.when(active)
                def _():
                    tree_copy(q, s, way, target).start()

        def update(r):
            cols = pl.ds(r * block, block)
            value = contract(x_all[q], fac_hi[cols], fac_lo[cols])
            if i == 1:
                part_copy(0, r).wait_recv()
                value = value + pre[r]
            part[i, r] = value
            if i < 3:
                part_copy(i, r).start()

        each_block(update)

    @pl.when(in_head)
    def _():
        out[:, :block] = x_own[...]

    def finish(r):
        cols = pl.ds(r * block, block)
        part_copy(2, r).wait_recv()
        part_copy(1, r).wait_recv()
        out[:, cols] = rhs[:, cols] - (part[3, r] + fin[r] + cross[r])
        for i in range(3):
            part_copy(i, r).wait_send()

    each_block(finish)

    for j in range(sections - 1):
        @pl.when((p > j) & in_head & (c == j))
        def _():
            for h in range(HALVES):
                l_copy(j, h, j ^ 2, 0).wait_send()
                l_copy(j, h, j ^ 1, 1).wait_send()

        @pl.when((p > j) & in_head & (c == (j ^ 2)))
        def _():
            for h in range(HALVES):
                l_forward(j, h).wait_send()

    @pl.when(in_head)
    def _():
        for s in range(SUBS):
            for target in range(1, sections):
                @pl.when(p < target)
                def _():
                    head_copy(s, target, p).wait_send()

            @pl.when(p != c)
            def _():
                gather_copy(s).wait_send()

    for q in order:
        for s in range(SUBS):
            for way, (active, target) in enumerate(links):
                @pl.when(active)
                def _():
                    tree_copy(q, s, way, target).wait_send()


def per_device(right_side, factor, inverses):
    width = right_side.shape[0]
    rows, block = factor.shape
    blocks = rows // block
    n_prow = lax.axis_size("prow")
    sections = lax.axis_size("pcol")
    f32, bf16 = jnp.float32, jnp.bfloat16
    vmem, dma = pltpu.VMEM, pltpu.SemaphoreType.DMA
    heads = sections - 1
    return pl.pallas_call(
        functools.partial(kernel, n_prow, sections),
        out_shape=jax.ShapeDtypeStruct(right_side.shape, f32),
        in_specs=[
            pl.BlockSpec(memory_space=pltpu.VMEM),
            pl.BlockSpec(memory_space=pl.ANY),
            pl.BlockSpec(memory_space=pl.ANY),
        ],
        out_specs=pl.BlockSpec(memory_space=pltpu.VMEM),
        scratch_shapes=[
            vmem((rows, block), f32), vmem((rows, block), bf16), vmem((rows, block), bf16),
            vmem((block, block), f32), vmem((block, block), bf16), vmem((block, block), bf16),
            vmem((heads, block, block), f32), vmem((heads, block, block), bf16), vmem((heads, block, block), bf16),
            vmem((width // SUBS, block), f32), vmem((width, block), f32),
            vmem((heads, width, block), f32), vmem((sections, width, block), f32),
            vmem((4, blocks, width, block), f32), vmem((blocks, width, block), f32),
            vmem((blocks, width, block), f32), vmem((blocks, width, block), f32),
            dma((2,)), dma((2, HALVES)), dma((heads, HALVES)), dma((heads, HALVES)),
            dma((sections, SUBS)), dma((heads, SUBS)), dma((SUBS,)),
            dma((3, sections, SUBS)), dma((sections, SUBS)), dma((3, blocks)),
            dma((blocks,)), dma((blocks,)), dma((blocks,)),
        ],
        compiler_params=pltpu.CompilerParams(
            collective_id=0, has_side_effects=True, vmem_limit_bytes=48 * 1024 * 1024
        ),
        name="solve_window",
    )(right_side, factor, inverses)


def solution(mesh):
    return jax.shard_map(
        per_device,
        mesh=mesh,
        in_specs=(P("pcol", "prow"), P("prow", "pcol"), P()),
        out_specs=P("pcol", "prow"),
        check_vma=False,
    )
```

time: 548 us -> 70.8 us (0.13)
  the two profiles are of different devices: /device:TPU:29 before, /device:TPU:25 now
where the time goes in v1:
time: 70.8 us; the launch traced here: 70.6 us
  Pallas kernels  67.2 us (95%)
  local copies, waits for them, and re-layouts  3.43 us (5%)
    pallas_call x1, Pallas kernels, per_device(): pl.pallas_call(functools.partial(kernel, n_prow, sections), out_shape=jax...  67.2 us
    unnamed x5, local copies, waits for them, and re-layouts  3.43 us

profile of v1, /device:TPU:25, one launch (start us, length us, event | category | flops | bytes accessed | tf_op | source)
XLA Modules:
  0.0 70.6 jit_solution(15214971361501737885)
XLA Ops:
  0.0 0.0 copy-start
  0.0 1.6 %copy-done = f32[1024,512]{1,0:T(8,128)S(1)} copy-done((f32[1024,512]{1,0:T(8,128)S(1)}, f32[1024,512]{1,0:T(8,128)}, u32[]{:S(2)}) %copy-start) | copy-done | bytes 2097176
  1.6 0.0 copy-start.1
  1.6 1.0 %copy-done.1 = f32[128,1024]{1,0:T(8,128)S(1)} copy-done((f32[128,1024]{1,0:T(8,128)S(1)}, f32[128,1024]{1,0:T(8,128)}, u32[]{:S(2)}) %copy-start.1) | copy-done | bytes 524312
  2.6 67.2 %solve_window.1 = f32[128,1024]{1,0:T(8,128)S(1)} custom-call(f32[128,1024]{1,0:T(8,128)S(1)} %copy-done.1, f32[1024,512]{1,0:T(8,128)S(1)} %copy-done, f32[2048,512]{1,0:T(8,128)} %inverses.1), custom_call_target="tpu_custom_call" | custom-call | tf_op jit(solution)/shard_map/solve_window/pallas_call | solution.py:257
  69.8 0.8 %copy.5 = f32[128,1024]{1,0:T(8,128)} copy(f32[128,1024]{1,0:T(8,128)S(1)} %solve_window.1) | data formatting | bytes 1048576
Async XLA Ops:
  0.0 1.6 %copy-start = (f32[1024,512]{1,0:T(8,128)S(1)}, f32[1024,512]{1,0:T(8,128)}, u32[]{:S(2)}) copy-start(f32[1024,512]{1,0:T(8,128)} %factor.1) | copy-start | bytes 6291460
  1.6 1.0 %copy-start.1 = (f32[128,1024]{1,0:T(8,128)S(1)}, f32[128,1024]{1,0:T(8,128)}, u32[]{:S(2)}) copy-start(f32[128,1024]{1,0:T(8,128)} %rhs.1) | copy-start | bytes 1572868

commit v2 on v1

v2 whole, which is shorter than its diff:
```python
import functools

import jax
import jax.numpy as jnp
from jax import lax
from jax.experimental import pallas as pl
from jax.experimental.pallas import tpu as pltpu
from jax.sharding import PartitionSpec as P

MESH = pl.DeviceIdType.MESH
SUBS = 2
HALVES = 2
PIECES = 4


def split(value):
    high = value.astype(jnp.bfloat16)
    low = (value - high.astype(jnp.float32)).astype(jnp.bfloat16)
    return high, low


def dot_nt(left, right):
    return lax.dot_general(left, right, (((1,), (1,)), ((), ())), preferred_element_type=jnp.float32)


def contract(left, right_high, right_low):
    rows = left.shape[0]
    high, low = split(left)
    both = dot_nt(jnp.concatenate([high, low], axis=0), right_high)
    return both[:rows] + (both[rows:] + dot_nt(high, right_low))


def kernel(
    n_prow, sections, rhs, factor, inverses, out,
    fac, dinv, d_hi, d_lo, l_in, l_hi, l_lo, l_oth,
    acc, x_own, x_head, x_all, part, fin,
    local_sem, l_send, l_fwd, l_recv, swap_send, swap_recv, head_send, head_recv,
    source_send, tree_send, x_recv, part_send, fin_recv,
):
    width = rhs.shape[0]
    block = factor.shape[1]
    piece = factor.shape[0] // PIECES
    p = lax.axis_index("prow")
    c = lax.axis_index("pcol")
    pair, parity = c // 2, c % 2
    mate = pair * 2 + 1 - parity
    over = (1 - pair) * 2 + parity
    z, x = p // 2, p % 2
    beside = z * 2 + 1 - x
    levels = n_prow // 2
    in_head = p < sections
    late = in_head & (p > 0) & (pair == 0)
    sub = width // SUBS
    half = block // HALVES

    fac_copy = pltpu.make_async_copy(factor, fac, local_sem.at[0])
    dinv_copy = pltpu.make_async_copy(
        inverses.at[pl.ds(lax.rem(p, sections) * block, block)], dinv, local_sem.at[1]
    )
    dinv_copy.start()
    fac_copy.start()

    barrier = pltpu.get_barrier_semaphore()
    above, below = lax.rem(p + 2, n_prow), lax.rem(p + n_prow - 2, n_prow)
    across = (z + 1 - 2 * (z % 2)) * 2 + 1 - x
    greeted = [(row, c) for row in (above, below, beside, across)]
    greeted += [(row, mate) for row in (above, below, beside)]
    greeted += [(p, lax.rem(c + step, sections)) for step in range(1, sections)]
    for device in greeted:
        pl.semaphore_signal(barrier, inc=1, device_id=device, device_id_type=MESH)
    pl.semaphore_wait(barrier, len(greeted))

    def send(src, dst, send_sem, recv_sem, row, col):
        return pltpu.make_async_remote_copy(
            src_ref=src, dst_ref=dst, send_sem=send_sem, recv_sem=recv_sem,
            device_id=(row, col), device_id_type=MESH,
        )

    def l_piece(j, h):
        return l_in.at[j, pl.ds(h * half, half)]

    def l_copy(j, h, target, way):
        return send(
            factor.at[pl.ds(h * half, half)], l_piece(j, h), l_send.at[way, h], l_recv.at[j, h], p, target
        )

    def l_forward(j, h):
        return send(l_piece(j, h), l_piece(j, h), l_fwd.at[j, h], l_recv.at[j, h], p, j ^ 3)

    def swap(m):
        rows = pl.ds(m * piece, piece)
        return send(factor.at[rows], l_oth.at[rows], swap_send.at[m], swap_recv.at[m], p, over)

    def each_piece(body):
        for m in range(PIECES):
            if m * piece < block:
                pl.when(p >= sections)(functools.partial(body, m))
            else:
                body(m)

    for j in range(sections - 1):
        @pl.when((p > j) & in_head & (c == j))
        def _():
            for h in range(HALVES):
                l_copy(j, h, j ^ 2, 0).start()
                l_copy(j, h, j ^ 1, 1).start()

    @pl.when(jnp.logical_not(late))
    def _():
        each_piece(lambda m: swap(m).start())

    dinv_copy.wait()
    d_hi[...], d_lo[...] = split(dinv[...])
    fac_copy.wait()

    for j in range(sections - 1):
        @pl.when((p > j) & in_head & (c == j))
        def _():
            l_hi[j], l_lo[j] = split(fac[:block])

        @pl.when((p > j) & in_head & (c == (j ^ 2)))
        def _():
            for h in range(HALVES):
                l_forward(j, h).wait_recv()
                l_forward(j, h).start()
            l_hi[j], l_lo[j] = split(l_in[j])

    for j in range(sections - 1):
        @pl.when((p > j) & in_head & ((c == (j ^ 1)) | (c == (j ^ 3))))
        def _():
            for h in range(HALVES):
                l_forward(j, h).wait_recv()
            l_hi[j], l_lo[j] = split(l_in[j])

    def head_copy(s, target, col):
        rows = pl.ds(s * sub, sub)
        return send(
            x_own.at[rows], x_head.at[col, rows], head_send.at[target, s], head_recv.at[col, s], target, c
        )

    root_col = pair * 2 + p % 2
    sources = (
        (z + 1 < levels, p + 2), (z > 0, p - 2), (z >= 0, beside), (c != root_col, p),
    )

    def source_copy(s, way, target):
        rows = pl.ds(s * sub, sub)
        return send(
            x_own.at[rows], x_all.at[p // 2, parity, rows],
            source_send.at[way, s], x_recv.at[p // 2, parity, s], target, root_col,
        )

    @pl.when(in_head)
    def _():
        for s in range(SUBS):
            rows = pl.ds(s * sub, sub)
            acc[...] = rhs[rows, :block]
            for j in range(sections - 1):
                @pl.when(j < p)
                def _():
                    head_copy(s, sections - 1, j).wait_recv()
                    acc[...] -= contract(x_head[j, rows], l_hi[j], l_lo[j])
            x_own[rows] = contract(acc[...], d_hi[...], d_lo[...])
            for target in range(1, sections):
                @pl.when(p < target)
                def _():
                    head_copy(s, target, p).start()
            for way, (active, target) in enumerate(sources):
                @pl.when(active)
                def _():
                    source_copy(s, way, target).start()

            @pl.when(c == root_col)
            def _():
                x_all[p // 2, parity, rows] = x_own[rows]

    for j in range(sections - 1):
        @pl.when((p > j) & in_head & (c == j))
        def _():
            for h in range(HALVES):
                l_copy(j, h, j ^ 2, 0).wait_send()

    @pl.when(late)
    def _():
        each_piece(lambda m: swap(m).start())

    def links(slot):
        on_line = (x == parity) & (z != slot)
        return (
            (on_line & (z > slot) & (z + 1 < levels), p + 2),
            (on_line & (z < slot) & (z > 0), p - 2),
            (on_line, beside),
        )

    def tree_copy(slot, side, s, way, target):
        ref = x_all.at[slot, side, pl.ds(s * sub, sub)]
        return send(ref, ref, tree_send.at[way, slot, side, s], x_recv.at[slot, side, s], target, c)

    def own_part(slot):
        def body(m):
            rows = pl.ds(m * piece, piece)
            value = contract(x_all[slot].reshape(2 * width, block), *split(fac[rows]))
            part[m] = value.reshape(2, width, piece)

        each_piece(body)

    for slot in range(2):
        for s in range(SUBS):
            for side in range(2):
                @pl.when((p != slot * 2 + parity) | (parity != side))
                def _():
                    tree_copy(slot, side, s, 2, beside).wait_recv()

                for way, (active, target) in enumerate(links(slot)):
                    @pl.when(active)
                    def _():
                        tree_copy(slot, side, s, way, target).start()

        pl.when(pair == slot)(functools.partial(own_part, slot))

    def part_copy(m):
        return send(part.at[m, 1 - parity], fin.at[m], part_send.at[m], fin_recv.at[m], p, mate)

    def other_part(m):
        swap(m).wait_recv()
        rows = pl.ds(m * piece, piece)
        value = contract(x_all[1 - pair].reshape(2 * width, block), *split(l_oth[rows]))
        part[m] += value.reshape(2, width, piece)
        part_copy(m).start()

    each_piece(other_part)

    @pl.when(in_head)
    def _():
        out[:, :block] = x_own[...]

    def finish(m):
        cols = pl.ds(m * piece, piece)
        part_copy(m).wait_recv()
        out[:, cols] = rhs[:, cols] - (part[m, parity] + fin[m])
        part_copy(m).wait_send()
        swap(m).wait_send()

    each_piece(finish)

    for j in range(sections - 1):
        @pl.when((p > j) & in_head & (c == j))
        def _():
            for h in range(HALVES):
                l_copy(j, h, j ^ 1, 1).wait_send()

        @pl.when((p > j) & in_head & (c == (j ^ 2)))
        def _():
            for h in range(HALVES):
                l_forward(j, h).wait_send()

    @pl.when(in_head)
    def _():
        for s in range(SUBS):
            for target in range(1, sections):
                @pl.when(p < target)
                def _():
                    head_copy(s, target, p).wait_send()
            for way, (active, target) in enumerate(sources):
                @pl.when(active)
                def _():
                    source_copy(s, way, target).wait_send()

    for slot in range(2):
        for s in range(SUBS):
            for side in range(2):
                for way, (active, target) in enumerate(links(slot)):
                    @pl.when(active)
                    def _():
                        tree_copy(slot, side, s, way, target).wait_send()


def per_device(right_side, factor, inverses):
    width = right_side.shape[0]
    rows, block = factor.shape
    n_prow = lax.axis_size("prow")
    sections = lax.axis_size("pcol")
    piece = rows // PIECES
    f32, bf16 = jnp.float32, jnp.bfloat16
    vmem, dma = pltpu.VMEM, pltpu.SemaphoreType.DMA
    heads = sections - 1
    return pl.pallas_call(
        functools.partial(kernel, n_prow, sections),
        out_shape=jax.ShapeDtypeStruct(right_side.shape, f32),
        in_specs=[
            pl.BlockSpec(memory_space=pltpu.VMEM),
            pl.BlockSpec(memory_space=pl.ANY),
            pl.BlockSpec(memory_space=pl.ANY),
        ],
        out_specs=pl.BlockSpec(memory_space=pltpu.VMEM),
        scratch_shapes=[
            vmem((rows, block), f32),
            vmem((block, block), f32), vmem((block, block), bf16), vmem((block, block), bf16),
            vmem((heads, block, block), f32), vmem((heads, block, block), bf16), vmem((heads, block, block), bf16),
            vmem((rows, block), f32),
            vmem((width // SUBS, block), f32), vmem((width, block), f32),
            vmem((heads, width, block), f32), vmem((2, 2, width, block), f32),
            vmem((PIECES, 2, width, piece), f32), vmem((PIECES, width, piece), f32),
            dma((2,)), dma((2, HALVES)), dma((heads, HALVES)), dma((heads, HALVES)),
            dma((PIECES,)), dma((PIECES,)),
            dma((sections, SUBS)), dma((heads, SUBS)),
            dma((4, SUBS)), dma((3, 2, 2, SUBS)), dma((2, 2, SUBS)), dma((PIECES,)), dma((PIECES,)),
        ],
        compiler_params=pltpu.CompilerParams(
            collective_id=0, has_side_effects=True, vmem_limit_bytes=60 * 1024 * 1024
        ),
        name="solve_window",
    )(right_side, factor, inverses)


def solution(mesh):
    return jax.shard_map(
        per_device,
        mesh=mesh,
        in_specs=(P("pcol", "prow"), P("prow", "pcol"), P()),
        out_specs=P("pcol", "prow"),
        check_vma=False,
    )
```

time: 70.8 us -> 71.4 us (level)
  the two profiles are of different devices: /device:TPU:25 before, /device:TPU:29 now
where the time goes in v2:
time: 71.4 us; the launch traced here: 71.2 us
  Pallas kernels  69.3 us (97%)
  local copies, waits for them, and re-layouts  1.89 us (3%)
    pallas_call x1, Pallas kernels, per_device(): pl.pallas_call(functools.partial(kernel, n_prow, sections), out_shape=jax...  69.3 us
    unnamed x1, local copies, waits for them, and re-layouts  1.89 us

profile of v2, /device:TPU:29, one launch (start us, length us, event | category | flops | bytes accessed | tf_op | source)
XLA Modules:
  0.0 71.2 jit_solution(16968426178405061956)
XLA Ops:
  0.0 69.3 %solve_window.1 = f32[128,1024]{1,0:T(8,128)} custom-call(f32[128,1024]{1,0:T(8,128)} %rhs.1, f32[1024,512]{1,0:T(8,128)} %factor.1, f32[2048,512]{1,0:T(8,128)} %inverses.1), custom_call_target="tpu_custom_call" | custom-call | tf_op jit(solution)/shard_map/solve_window/pallas_call | solution.py:287
  69.3 1.9 %copy.5 = f32[128,1024]{1,0:T(8,128)} copy(f32[128,1024]{1,0:T(8,128)} %solve_window.1) | data formatting | bytes 1048576

commit v3 on v2

--- a/solution.py
+++ b/solution.py
@@ -32,10 +32,10 @@
 
 def kernel(
     n_prow, sections, rhs, factor, inverses, out,
-    fac, dinv, d_hi, d_lo, l_in, l_hi, l_lo, l_oth,
-    acc, x_own, x_head, x_all, part, fin,
+    fac, f_hi, f_lo, dinv, d_hi, d_lo, l_in, l_hi, l_lo, l_oth,
+    acc, x_own, x_head, x_all, x_split, part, fin,
     local_sem, l_send, l_fwd, l_recv, swap_send, swap_recv, head_send, head_recv,
-    source_send, tree_send, x_recv, part_send, fin_recv,
+    mate_send, up_send, back_send, tree_send, x_recv, part_send, fin_recv,
 ):
     width = rhs.shape[0]
     block = factor.shape[1]
@@ -64,7 +64,7 @@
     above, below = lax.rem(p + 2, n_prow), lax.rem(p + n_prow - 2, n_prow)
     across = (z + 1 - 2 * (z % 2)) * 2 + 1 - x
     greeted = [(row, c) for row in (above, below, beside, across)]
-    greeted += [(row, mate) for row in (above, below, beside)]
+    greeted += [(row, mate) for row in (above, below, beside, across)]
     greeted += [(p, lax.rem(c + step, sections)) for step in range(1, sections)]
     for device in greeted:
         pl.semaphore_signal(barrier, inc=1, device_id=device, device_id_type=MESH)
@@ -138,17 +138,32 @@
             x_own.at[rows], x_head.at[col, rows], head_send.at[target, s], head_recv.at[col, s], target, c
         )
 
-    root_col = pair * 2 + p % 2
-    sources = (
-        (z + 1 < levels, p + 2), (z > 0, p - 2), (z >= 0, beside), (c != root_col, p),
-    )
-
-    def source_copy(s, way, target):
+    def publish_copy(ref, k, s, sems, row):
         rows = pl.ds(s * sub, sub)
         return send(
-            x_own.at[rows], x_all.at[p // 2, parity, rows],
-            source_send.at[way, s], x_recv.at[p // 2, parity, s], target, root_col,
-        )
+            ref.at[rows], x_all.at[k // 2, parity, rows],
+            sems, x_recv.at[k // 2, parity, s], row, pair * 2 + k % 2,
+        )
+
+    def publish(ref, k, s, act):
+        pl.when(parity != k % 2)(lambda: act(publish_copy(ref, k, s, mate_send.at[k, s], p)))
+        pl.when((p == 2 + k % 2) & (z + 1 < levels))(
+            lambda: act(publish_copy(ref, k, s, up_send.at[k, s], p + 2))
+        )
+
+    def keep(ref, k, s):
+        rows = pl.ds(s * sub, sub)
+
+        @pl.when(parity == k % 2)
+        def _():
+            x_all[k // 2, parity, rows] = ref[rows]
+
+    def go_back(s, act):
+        for row in range(sections - 1):
+            pl.when(row < p)(lambda: act(publish_copy(x_own, p, s, back_send.at[row, s], row)))
+
+    start = lambda copy: copy.start()
+    drain = lambda copy: copy.wait_send()
 
     @pl.when(in_head)
     def _():
@@ -159,20 +174,23 @@
                 @pl.when(j < p)
                 def _():
                     head_copy(s, sections - 1, j).wait_recv()
+                    publish(x_head.at[j], j, s, start)
                     acc[...] -= contract(x_head[j, rows], l_hi[j], l_lo[j])
             x_own[rows] = contract(acc[...], d_hi[...], d_lo[...])
             for target in range(1, sections):
-                @pl.when(p < target)
+                @pl.when((p == target - 1) | ((p < target) & (target < sections - 1)))
                 def _():
                     head_copy(s, target, p).start()
-            for way, (active, target) in enumerate(sources):
-                @pl.when(active)
-                def _():
-                    source_copy(s, way, target).start()
-
-            @pl.when(c == root_col)
-            def _():
-                x_all[p // 2, parity, rows] = x_own[rows]
+            publish(x_own, p, s, start)
+            go_back(s, start)
+            keep(x_own, p, s)
+            for j in range(sections - 1):
+                pl.when(j < p)(lambda: keep(x_head.at[j], j, s))
+
+        @pl.when(p < sections - 2)
+        def _():
+            for s in range(SUBS):
+                head_copy(s, sections - 1, p).start()
 
     for j in range(sections - 1):
         @pl.when((p > j) & in_head & (c == j))
@@ -184,51 +202,82 @@
     def _():
         each_piece(lambda m: swap(m).start())
 
-    def links(slot):
-        on_line = (x == parity) & (z != slot)
-        return (
-            (on_line & (z > slot) & (z + 1 < levels), p + 2),
-            (on_line & (z < slot) & (z > 0), p - 2),
-            (on_line, beside),
-        )
+    for m in range(PIECES):
+        rows = pl.ds(m * piece, piece)
+        f_hi[rows], f_lo[rows] = split(fac[rows])
+
+    links = (
+        (jnp.logical_not(in_head) & (x == parity) & (z + 1 < levels), p + 2),
+        (jnp.logical_not(in_head) & (x == parity), beside),
+    )
 
     def tree_copy(slot, side, s, way, target):
         ref = x_all.at[slot, side, pl.ds(s * sub, sub)]
         return send(ref, ref, tree_send.at[way, slot, side, s], x_recv.at[slot, side, s], target, c)
 
-    def own_part(slot):
-        def body(m):
-            rows = pl.ds(m * piece, piece)
-            value = contract(x_all[slot].reshape(2 * width, block), *split(fac[rows]))
-            part[m] = value.reshape(2, width, piece)
-
-        each_piece(body)
-
-    for slot in range(2):
+    def spread(slot):
+        kept = in_head & (p >= slot * 2 + parity)
         for s in range(SUBS):
             for side in range(2):
-                @pl.when((p != slot * 2 + parity) | (parity != side))
+                @pl.when(jnp.logical_not(kept & (parity == side)))
                 def _():
-                    tree_copy(slot, side, s, 2, beside).wait_recv()
-
-                for way, (active, target) in enumerate(links(slot)):
+                    tree_copy(slot, side, s, 1, beside).wait_recv()
+
+                for way, (active, target) in enumerate(links):
                     @pl.when(active)
                     def _():
                         tree_copy(slot, side, s, way, target).start()
-
-        pl.when(pair == slot)(functools.partial(own_part, slot))
+        high, low = split(x_all[slot].reshape(2 * width, block))
+        x_split[slot, :2 * width] = high
+        x_split[slot, 2 * width:] = low
+
+    def product(slot, right_high, right_low):
+        both = dot_nt(x_split[slot], right_high)
+        low = dot_nt(x_split[slot, :2 * width], right_low)
+        return (both[:2 * width] + (both[2 * width:] + low)).reshape(2, width, piece)
+
+    def own(m, slot):
+        rows = pl.ds(m * piece, piece)
+        return product(slot, f_hi[rows], f_lo[rows])
+
+    def other(m, slot):
+        swap(m).wait_recv()
+        return product(slot, *split(l_oth[pl.ds(m * piece, piece)]))
 
     def part_copy(m):
         return send(part.at[m, 1 - parity], fin.at[m], part_send.at[m], fin_recv.at[m], p, mate)
 
-    def other_part(m):
-        swap(m).wait_recv()
-        rows = pl.ds(m * piece, piece)
-        value = contract(x_all[1 - pair].reshape(2 * width, block), *split(l_oth[rows]))
-        part[m] += value.reshape(2, width, piece)
+    def first_own(slot, m):
+        part[m] = own(m, slot)
+
+    def first_other(m):
+        if m < PIECES - 1:
+            part[m] = other(m, 0)
+
+    def then_own(m):
+        if m < PIECES - 1:
+            part[m] += own(m, 1)
+        else:
+            part[m] = own(m, 1)
+            part[m] += other(m, 0)
         part_copy(m).start()
 
-    each_piece(other_part)
+    def then_other(slot, m):
+        part[m] += other(m, slot)
+        part_copy(m).start()
+
+    early = (pair == 1) & (in_head | (x != parity))
+    spread(0)
+    pl.when(pair == 0)(lambda: each_piece(functools.partial(first_own, 0)))
+    pl.when(early)(lambda: each_piece(first_other))
+    spread(1)
+    pl.when(pair == 0)(lambda: each_piece(functools.partial(then_other, 1)))
+    pl.when(early)(lambda: each_piece(then_own))
+
+    @pl.when((pair == 1) & jnp.logical_not(early))
+    def _():
+        each_piece(functools.partial(first_own, 1))
+        each_piece(functools.partial(then_other, 0))
 
     @pl.when(in_head)
     def _():
@@ -261,15 +310,15 @@
                 @pl.when(p < target)
                 def _():
                     head_copy(s, target, p).wait_send()
-            for way, (active, target) in enumerate(sources):
-                @pl.when(active)
-                def _():
-                    source_copy(s, way, target).wait_send()
+            publish(x_own, p, s, drain)
+            go_back(s, drain)
+            for j in range(sections - 1):
+                pl.when(j < p)(lambda: publish(x_head.at[j], j, s, drain))
 
     for slot in range(2):
         for s in range(SUBS):
             for side in range(2):
-                for way, (active, target) in enumerate(links(slot)):
+                for way, (active, target) in enumerate(links):
                     @pl.when(active)
                     def _():
                         tree_copy(slot, side, s, way, target).wait_send()
@@ -294,17 +343,19 @@
         ],
         out_specs=pl.BlockSpec(memory_space=pltpu.VMEM),
         scratch_shapes=[
-            vmem((rows, block), f32),
+            vmem((rows, block), f32), vmem((rows, block), bf16), vmem((rows, block), bf16),
             vmem((block, block), f32), vmem((block, block), bf16), vmem((block, block), bf16),
             vmem((heads, block, block), f32), vmem((heads, block, block), bf16), vmem((heads, block, block), bf16),
             vmem((rows, block), f32),
             vmem((width // SUBS, block), f32), vmem((width, block), f32),
             vmem((heads, width, block), f32), vmem((2, 2, width, block), f32),
+            vmem((2, 4 * width, block), bf16),
             vmem((PIECES, 2, width, piece), f32), vmem((PIECES, width, piece), f32),
             dma((2,)), dma((2, HALVES)), dma((heads, HALVES)), dma((heads, HALVES)),
             dma((PIECES,)), dma((PIECES,)),
             dma((sections, SUBS)), dma((heads, SUBS)),
-            dma((4, SUBS)), dma((3, 2, 2, SUBS)), dma((2, 2, SUBS)), dma((PIECES,)), dma((PIECES,)),
+            dma((sections, SUBS)), dma((sections, SUBS)), dma((heads, SUBS)),
+            dma((2, 2, 2, SUBS)), dma((2, 2, SUBS)), dma((PIECES,)), dma((PIECES,)),
         ],
         compiler_params=pltpu.CompilerParams(
             collective_id=0, has_side_effects=True, vmem_limit_bytes=60 * 1024 * 1024

time: 71.4 us -> 63.5 us (0.89)
  Pallas kernels: 69.3 us -> 61.4 us
    pallas_call x1, Pallas kernels: 69.3 us -> 61.4 us  [per_device(): pl.pallas_call(functools.partial(kernel, n_prow, sections), out_shape=jax...]
where the time goes in v3:
time: 63.5 us; the launch traced here: 63.3 us
  Pallas kernels  61.4 us (97%)
  local copies, waits for them, and re-layouts  1.89 us (3%)
    pallas_call x1, Pallas kernels, per_device(): pl.pallas_call(functools.partial(kernel, n_prow, sections), out_shape=jax...  61.4 us
    unnamed x1, local copies, waits for them, and re-layouts  1.89 us

profile of v3, /device:TPU:29, one launch (start us, length us, event | category | flops | bytes accessed | tf_op | source)
XLA Modules:
  0.0 63.3 jit_solution(13561239722796844057)
XLA Ops:
  0.0 61.4 %solve_window.1 = f32[128,1024]{1,0:T(8,128)} custom-call(f32[128,1024]{1,0:T(8,128)} %rhs.1, f32[1024,512]{1,0:T(8,128)} %factor.1, f32[2048,512]{1,0:T(8,128)} %inverses.1), custom_call_target="tpu_custom_call" | custom-call | tf_op jit(solution)/shard_map/solve_window/pallas_call | solution.py:336
  61.4 1.9 %copy.5 = f32[128,1024]{1,0:T(8,128)} copy(f32[128,1024]{1,0:T(8,128)} %solve_window.1) | data formatting | bytes 1048576

commit v4 on v3

--- a/solution.py
+++ b/solution.py
@@ -23,6 +23,10 @@
     return lax.dot_general(left, right, (((1,), (1,)), ((), ())), preferred_element_type=jnp.float32)
 
 
+def dot_nn(left, right):
+    return lax.dot_general(left, right, (((1,), (0,)), ((), ())), preferred_element_type=jnp.float32)
+
+
 def contract(left, right_high, right_low):
     rows = left.shape[0]
     high, low = split(left)
@@ -32,7 +36,7 @@
 
 def kernel(
     n_prow, sections, rhs, factor, inverses, out,
-    fac, f_hi, f_lo, dinv, d_hi, d_lo, l_in, l_hi, l_lo, l_oth,
+    fac, f_hi, f_lo, dinv, d_hi, d_lo, l_in, l_hi, l_lo, m_hi, m_lo, l_oth,
     acc, x_own, x_head, x_all, x_split, part, fin,
     local_sem, l_send, l_fwd, l_recv, swap_send, swap_recv, head_send, head_recv,
     mate_send, up_send, back_send, tree_send, x_recv, part_send, fin_recv,
@@ -49,7 +53,8 @@
     beside = z * 2 + 1 - x
     levels = n_prow // 2
     in_head = p < sections
-    late = in_head & (p > 0) & (pair == 0)
+    last = sections - 1
+    at_once = (p >= sections) | ((p == last - 1) & (pair == 1))
     sub = width // SUBS
     half = block // HALVES
 
@@ -105,7 +110,7 @@
                 l_copy(j, h, j ^ 2, 0).start()
                 l_copy(j, h, j ^ 1, 1).start()
 
-    @pl.when(jnp.logical_not(late))
+    @pl.when(at_once)
     def _():
         each_piece(lambda m: swap(m).start())
 
@@ -165,42 +170,67 @@
     start = lambda copy: copy.start()
     drain = lambda copy: copy.wait_send()
 
+    def swap_late():
+        for j in range(sections - 1):
+            @pl.when((p > j) & (c == j))
+            def _():
+                for h in range(HALVES):
+                    l_copy(j, h, j ^ 2, 0).wait_send()
+        each_piece(lambda m: swap(m).start())
+
+    pl.when(p == last)(swap_late)
+
     @pl.when(in_head)
     def _():
+        acc[...] = rhs[:, :block]
+        for j in range(sections - 1):
+            @pl.when(p == j + 1)
+            def _():
+                both = dot_nn(jnp.concatenate([d_hi[...], d_lo[...]], axis=0), l_hi[j])
+                chain = both[:block] + (both[block:] + dot_nn(d_hi[...], l_lo[j]))
+                m_hi[...], m_lo[...] = split(chain)
+
+        for j in range(sections - 2):
+            @pl.when(p > j + 1)
+            def _():
+                for s in range(SUBS):
+                    head_copy(s, last, j).wait_recv()
+                    publish(x_head.at[j], j, s, start)
+                acc[...] -= contract(x_head[j], l_hi[j], l_lo[j])
+
+        acc[...] = contract(acc[...], d_hi[...], d_lo[...])
         for s in range(SUBS):
             rows = pl.ds(s * sub, sub)
-            acc[...] = rhs[rows, :block]
+            x_own[rows] = acc[rows]
             for j in range(sections - 1):
-                @pl.when(j < p)
+                @pl.when(p == j + 1)
                 def _():
-                    head_copy(s, sections - 1, j).wait_recv()
-                    publish(x_head.at[j], j, s, start)
-                    acc[...] -= contract(x_head[j, rows], l_hi[j], l_lo[j])
-            x_own[rows] = contract(acc[...], d_hi[...], d_lo[...])
+                    head_copy(s, last, j).wait_recv()
+                    x_own[rows] = acc[rows] - contract(x_head[j, rows], m_hi[...], m_lo[...])
             for target in range(1, sections):
                 @pl.when((p == target - 1) | ((p < target) & (target < sections - 1)))
                 def _():
                     head_copy(s, target, p).start()
             publish(x_own, p, s, start)
             go_back(s, start)
+            for j in range(sections - 1):
+                @pl.when(p == j + 1)
+                def _():
+                    publish(x_head.at[j], j, s, start)
+
+        @pl.when(p < sections - 2)
+        def _():
+            for s in range(SUBS):
+                head_copy(s, sections - 1, p).start()
+
+        for s in range(SUBS):
             keep(x_own, p, s)
             for j in range(sections - 1):
                 pl.when(j < p)(lambda: keep(x_head.at[j], j, s))
 
-        @pl.when(p < sections - 2)
-        def _():
-            for s in range(SUBS):
-                head_copy(s, sections - 1, p).start()
-
-    for j in range(sections - 1):
-        @pl.when((p > j) & in_head & (c == j))
-        def _():
-            for h in range(HALVES):
-                l_copy(j, h, j ^ 2, 0).wait_send()
-
-    @pl.when(late)
-    def _():
-        each_piece(lambda m: swap(m).start())
+    @pl.when(jnp.logical_not(at_once) & (p != last))
+    def _():
+        swap_late()
 
     for m in range(PIECES):
         rows = pl.ds(m * piece, piece)
@@ -346,8 +376,8 @@
             vmem((rows, block), f32), vmem((rows, block), bf16), vmem((rows, block), bf16),
             vmem((block, block), f32), vmem((block, block), bf16), vmem((block, block), bf16),
             vmem((heads, block, block), f32), vmem((heads, block, block), bf16), vmem((heads, block, block), bf16),
-            vmem((rows, block), f32),
-            vmem((width // SUBS, block), f32), vmem((width, block), f32),
+            vmem((block, block), bf16), vmem((block, block), bf16), vmem((rows, block), f32),
+            vmem((width, block), f32), vmem((width, block), f32),
             vmem((heads, width, block), f32), vmem((2, 2, width, block), f32),
             vmem((2, 4 * width, block), bf16),
             vmem((PIECES, 2, width, piece), f32), vmem((PIECES, width, piece), f32),

time: 63.5 us -> 62 us (0.976)
  Pallas kernels: 61.4 us -> 59.9 us
    pallas_call x1, Pallas kernels: 61.4 us -> 59.9 us  [per_device(): pl.pallas_call(functools.partial(kernel, n_prow, sections), out_shape=jax...]
where the time goes in v4:
time: 62 us; the launch traced here: 61.8 us
  Pallas kernels  59.9 us (97%)
  local copies, waits for them, and re-layouts  1.89 us (3%)
    pallas_call x1, Pallas kernels, per_device(): pl.pallas_call(functools.partial(kernel, n_prow, sections), out_shape=jax...  59.9 us
    unnamed x1, local copies, waits for them, and re-layouts  1.89 us

profile of v4, /device:TPU:29, one launch (start us, length us, event | category | flops | bytes accessed | tf_op | source)
XLA Modules:
  0.0 61.8 jit_solution(7659311059687933214)
XLA Ops:
  0.0 59.9 %solve_window.1 = f32[128,1024]{1,0:T(8,128)} custom-call(f32[128,1024]{1,0:T(8,128)} %rhs.1, f32[1024,512]{1,0:T(8,128)} %factor.1, f32[2048,512]{1,0:T(8,128)} %inverses.1), custom_call_target="tpu_custom_call" | custom-call | tf_op jit(solution)/shard_map/solve_window/pallas_call | solution.py:366
  59.9 1.9 %copy.5 = f32[128,1024]{1,0:T(8,128)} copy(f32[128,1024]{1,0:T(8,128)} %solve_window.1) | data formatting | bytes 1048576

commit v5 on v4

--- a/solution.py
+++ b/solution.py
@@ -54,6 +54,7 @@
     levels = n_prow // 2
     in_head = p < sections
     last = sections - 1
+    folded = (pair == 0) | (p == last)
     at_once = (p >= sections) | ((p == last - 1) & (pair == 1))
     sub = width // SUBS
     half = block // HALVES
@@ -110,9 +111,14 @@
                 l_copy(j, h, j ^ 2, 0).start()
                 l_copy(j, h, j ^ 1, 1).start()
 
+    first, rest = range(PIECES // 2), range(PIECES // 2, PIECES)
+
     @pl.when(at_once)
     def _():
-        each_piece(lambda m: swap(m).start())
+        for m in first:
+            pl.when(p >= sections)(lambda: swap(m).start())
+        for m in rest:
+            pl.when(p < sections)(lambda: swap(m).start())
 
     dinv_copy.wait()
     d_hi[...], d_lo[...] = split(dinv[...])
@@ -184,14 +190,14 @@
     def _():
         acc[...] = rhs[:, :block]
         for j in range(sections - 1):
-            @pl.when(p == j + 1)
+            @pl.when((p == j + 1) & folded)
             def _():
                 both = dot_nn(jnp.concatenate([d_hi[...], d_lo[...]], axis=0), l_hi[j])
                 chain = both[:block] + (both[block:] + dot_nn(d_hi[...], l_lo[j]))
                 m_hi[...], m_lo[...] = split(chain)
 
-        for j in range(sections - 2):
-            @pl.when(p > j + 1)
+        for j in range(sections - 1):
+            @pl.when((p > j + 1) | ((p == j + 1) & jnp.logical_not(folded)))
             def _():
                 for s in range(SUBS):
                     head_copy(s, last, j).wait_recv()
@@ -203,7 +209,7 @@
             rows = pl.ds(s * sub, sub)
             x_own[rows] = acc[rows]
             for j in range(sections - 1):
-                @pl.when(p == j + 1)
+                @pl.when((p == j + 1) & folded)
                 def _():
                     head_copy(s, last, j).wait_recv()
                     x_own[rows] = acc[rows] - contract(x_head[j, rows], m_hi[...], m_lo[...])
@@ -214,7 +220,7 @@
             publish(x_own, p, s, start)
             go_back(s, start)
             for j in range(sections - 1):
-                @pl.when(p == j + 1)
+                @pl.when((p == j + 1) & folded)
                 def _():
                     publish(x_head.at[j], j, s, start)
 
@@ -280,34 +286,39 @@
     def first_own(slot, m):
         part[m] = own(m, slot)
 
-    def first_other(m):
-        if m < PIECES - 1:
-            part[m] = other(m, 0)
-
-    def then_own(m):
-        if m < PIECES - 1:
-            part[m] += own(m, 1)
-        else:
-            part[m] = own(m, 1)
-            part[m] += other(m, 0)
-        part_copy(m).start()
-
     def then_other(slot, m):
         part[m] += other(m, slot)
         part_copy(m).start()
 
-    early = (pair == 1) & (in_head | (x != parity))
+    def then_own(m):
+        if m in first:
+            part[m] += own(m, 1)
+            part_copy(m).start()
+        else:
+            part[m] = own(m, 1)
+
+    @pl.when(p >= sections)
+    def _():
+        for m in first:
+            swap(m).wait_send()
+            swap(m + PIECES // 2).start()
+
     spread(0)
     pl.when(pair == 0)(lambda: each_piece(functools.partial(first_own, 0)))
-    pl.when(early)(lambda: each_piece(first_other))
+
+    @pl.when((pair == 1) & (p >= sections))
+    def _():
+        for m in first:
+            part[m] = other(m, 0)
+
     spread(1)
     pl.when(pair == 0)(lambda: each_piece(functools.partial(then_other, 1)))
-    pl.when(early)(lambda: each_piece(then_own))
-
-    @pl.when((pair == 1) & jnp.logical_not(early))
-    def _():
-        each_piece(functools.partial(first_own, 1))
-        each_piece(functools.partial(then_other, 0))
+
+    @pl.when(pair == 1)
+    def _():
+        each_piece(then_own)
+        for m in rest:
+            then_other(0, m)
 
     @pl.when(in_head)
     def _():
@@ -318,7 +329,8 @@
         part_copy(m).wait_recv()
         out[:, cols] = rhs[:, cols] - (part[m, parity] + fin[m])
         part_copy(m).wait_send()
-        swap(m).wait_send()
+        if m in rest:
+            swap(m).wait_send()
 
     each_piece(finish)
 

time: 62 us -> 61.2 us (0.987)
  Pallas kernels: 59.9 us -> 59.1 us
    pallas_call x1, Pallas kernels: 59.9 us -> 59.1 us  [per_device(): pl.pallas_call(functools.partial(kernel, n_prow, sections), out_shape=jax...]
where the time goes in v5:
time: 61.2 us; the launch traced here: 61 us
  Pallas kernels  59.1 us (97%)
  local copies, waits for them, and re-layouts  1.89 us (3%)
    pallas_call x1, Pallas kernels, per_device(): pl.pallas_call(functools.partial(kernel, n_prow, sections), out_shape=jax...  59.1 us
    unnamed x1, local copies, waits for them, and re-layouts  1.89 us

profile of v5, /device:TPU:29, one launch (start us, length us, event | category | flops | bytes accessed | tf_op | source)
XLA Modules:
  0.0 61.0 jit_solution(17904549408227490898)
XLA Ops:
  0.0 59.1 %solve_window.1 = f32[128,1024]{1,0:T(8,128)} custom-call(f32[128,1024]{1,0:T(8,128)} %rhs.1, f32[1024,512]{1,0:T(8,128)} %factor.1, f32[2048,512]{1,0:T(8,128)} %inverses.1), custom_call_target="tpu_custom_call" | custom-call | tf_op jit(solution)/shard_map/solve_window/pallas_call | solution.py:378
  59.1 1.9 %copy.5 = f32[128,1024]{1,0:T(8,128)} copy(f32[128,1024]{1,0:T(8,128)} %solve_window.1) | data formatting | bytes 1048576

commit v6 on v5

--- a/solution.py
+++ b/solution.py
@@ -120,62 +120,6 @@
         for m in rest:
             pl.when(p < sections)(lambda: swap(m).start())
 
-    dinv_copy.wait()
-    d_hi[...], d_lo[...] = split(dinv[...])
-    fac_copy.wait()
-
-    for j in range(sections - 1):
-        @pl.when((p > j) & in_head & (c == j))
-        def _():
-            l_hi[j], l_lo[j] = split(fac[:block])
-
-        @pl.when((p > j) & in_head & (c == (j ^ 2)))
-        def _():
-            for h in range(HALVES):
-                l_forward(j, h).wait_recv()
-                l_forward(j, h).start()
-            l_hi[j], l_lo[j] = split(l_in[j])
-
-    for j in range(sections - 1):
-        @pl.when((p > j) & in_head & ((c == (j ^ 1)) | (c == (j ^ 3))))
-        def _():
-            for h in range(HALVES):
-                l_forward(j, h).wait_recv()
-            l_hi[j], l_lo[j] = split(l_in[j])
-
-    def head_copy(s, target, col):
-        rows = pl.ds(s * sub, sub)
-        return send(
-            x_own.at[rows], x_head.at[col, rows], head_send.at[target, s], head_recv.at[col, s], target, c
-        )
-
-    def publish_copy(ref, k, s, sems, row):
-        rows = pl.ds(s * sub, sub)
-        return send(
-            ref.at[rows], x_all.at[k // 2, parity, rows],
-            sems, x_recv.at[k // 2, parity, s], row, pair * 2 + k % 2,
-        )
-
-    def publish(ref, k, s, act):
-        pl.when(parity != k % 2)(lambda: act(publish_copy(ref, k, s, mate_send.at[k, s], p)))
-        pl.when((p == 2 + k % 2) & (z + 1 < levels))(
-            lambda: act(publish_copy(ref, k, s, up_send.at[k, s], p + 2))
-        )
-
-    def keep(ref, k, s):
-        rows = pl.ds(s * sub, sub)
-
-        @pl.when(parity == k % 2)
-        def _():
-            x_all[k // 2, parity, rows] = ref[rows]
-
-    def go_back(s, act):
-        for row in range(sections - 1):
-            pl.when(row < p)(lambda: act(publish_copy(x_own, p, s, back_send.at[row, s], row)))
-
-    start = lambda copy: copy.start()
-    drain = lambda copy: copy.wait_send()
-
     def swap_late():
         for j in range(sections - 1):
             @pl.when((p > j) & (c == j))
@@ -184,7 +128,64 @@
                     l_copy(j, h, j ^ 2, 0).wait_send()
         each_piece(lambda m: swap(m).start())
 
-    pl.when(p == last)(swap_late)
+    dinv_copy.wait()
+    d_hi[...], d_lo[...] = split(dinv[...])
+    fac_copy.wait()
+    pl.when((p == last) & (pair == 1))(swap_late)
+
+    for j in range(sections - 1):
+        @pl.when((p > j) & in_head & (c == j))
+        def _():
+            l_hi[j], l_lo[j] = split(fac[:block])
+
+        @pl.when((p > j) & in_head & (c == (j ^ 2)))
+        def _():
+            for h in range(HALVES):
+                l_forward(j, h).wait_recv()
+                l_forward(j, h).start()
+            l_hi[j], l_lo[j] = split(l_in[j])
+
+    for j in range(sections - 1):
+        @pl.when((p > j) & in_head & ((c == (j ^ 1)) | (c == (j ^ 3))))
+        def _():
+            for h in range(HALVES):
+                l_forward(j, h).wait_recv()
+            l_hi[j], l_lo[j] = split(l_in[j])
+
+    def head_copy(s, target, col):
+        rows = pl.ds(s * sub, sub)
+        return send(
+            x_own.at[rows], x_head.at[col, rows], head_send.at[target, s], head_recv.at[col, s], target, c
+        )
+
+    def publish_copy(ref, k, s, sems, row):
+        rows = pl.ds(s * sub, sub)
+        return send(
+            ref.at[rows], x_all.at[k // 2, parity, rows],
+            sems, x_recv.at[k // 2, parity, s], row, pair * 2 + k % 2,
+        )
+
+    def publish(ref, k, s, act):
+        pl.when(parity != k % 2)(lambda: act(publish_copy(ref, k, s, mate_send.at[k, s], p)))
+        pl.when((p == 2 + k % 2) & (z + 1 < levels))(
+            lambda: act(publish_copy(ref, k, s, up_send.at[k, s], p + 2))
+        )
+
+    def keep(ref, k, s):
+        rows = pl.ds(s * sub, sub)
+
+        @pl.when(parity == k % 2)
+        def _():
+            x_all[k // 2, parity, rows] = ref[rows]
+
+    def go_back(s, act):
+        for row in range(sections - 1):
+            pl.when(row < p)(lambda: act(publish_copy(x_own, p, s, back_send.at[row, s], row)))
+
+    start = lambda copy: copy.start()
+    drain = lambda copy: copy.wait_send()
+
+    pl.when((p == last) & (pair == 0))(swap_late)
 
     @pl.when(in_head)
     def _():
@@ -218,7 +219,6 @@
                 def _():
                     head_copy(s, target, p).start()
             publish(x_own, p, s, start)
-            go_back(s, start)
             for j in range(sections - 1):
                 @pl.when((p == j + 1) & folded)
                 def _():
@@ -228,6 +228,9 @@
         def _():
             for s in range(SUBS):
                 head_copy(s, sections - 1, p).start()
+
+        for s in range(SUBS):
+            go_back(s, start)
 
         for s in range(SUBS):
             keep(x_own, p, s)
@@ -290,10 +293,13 @@
         part[m] += other(m, slot)
         part_copy(m).start()
 
-    def then_own(m):
+    def whole_own(m):
+        part[m] += own(m, 1)
+        part_copy(m).start()
+
+    def late_own(m):
         if m in first:
-            part[m] += own(m, 1)
-            part_copy(m).start()
+            whole_own(m)
         else:
             part[m] = own(m, 1)
 
@@ -303,6 +309,7 @@
             swap(m).wait_send()
             swap(m + PIECES // 2).start()
 
+    leaf = jnp.logical_not(in_head) & (x != parity)
     spread(0)
     pl.when(pair == 0)(lambda: each_piece(functools.partial(first_own, 0)))
 
@@ -311,12 +318,21 @@
         for m in first:
             part[m] = other(m, 0)
 
+    @pl.when((pair == 1) & leaf)
+    def _():
+        for m in rest:
+            part[m] = other(m, 0)
+
     spread(1)
     pl.when(pair == 0)(lambda: each_piece(functools.partial(then_other, 1)))
 
-    @pl.when(pair == 1)
-    def _():
-        each_piece(then_own)
+    @pl.when((pair == 1) & leaf)
+    def _():
+        each_piece(whole_own)
+
+    @pl.when((pair == 1) & jnp.logical_not(leaf))
+    def _():
+        each_piece(late_own)
         for m in rest:
             then_other(0, m)
 

time: 61.2 us -> 60.5 us (0.989)
  Pallas kernels: 59.1 us -> 58.4 us
    pallas_call x1, Pallas kernels: 59.1 us -> 58.4 us  [per_device(): pl.pallas_call(functools.partial(kernel, n_prow, sections), out_shape=jax...]
where the time goes in v6:
time: 60.5 us; the launch traced here: 60.3 us
  Pallas kernels  58.4 us (97%)
  local copies, waits for them, and re-layouts  1.89 us (3%)
    pallas_call x1, Pallas kernels, per_device(): pl.pallas_call(functools.partial(kernel, n_prow, sections), out_shape=jax...  58.4 us
    unnamed x1, local copies, waits for them, and re-layouts  1.89 us

profile of v6, /device:TPU:29, one launch (start us, length us, event | category | flops | bytes accessed | tf_op | source)
XLA Modules:
  0.0 60.3 jit_solution(8715506064005275007)
XLA Ops:
  0.0 58.4 %solve_window.1 = f32[128,1024]{1,0:T(8,128)} custom-call(f32[128,1024]{1,0:T(8,128)} %rhs.1, f32[1024,512]{1,0:T(8,128)} %factor.1, f32[2048,512]{1,0:T(8,128)} %inverses.1), custom_call_target="tpu_custom_call" | custom-call | tf_op jit(solution)/shard_map/solve_window/pallas_call | solution.py:394
  58.5 1.9 %copy.5 = f32[128,1024]{1,0:T(8,128)} copy(f32[128,1024]{1,0:T(8,128)} %solve_window.1) | data formatting | bytes 1048576

commit v7 on v6

--- a/solution.py
+++ b/solution.py
@@ -107,8 +107,8 @@
     for j in range(sections - 1):
         @pl.when((p > j) & in_head & (c == j))
         def _():
-            for h in range(HALVES):
-                l_copy(j, h, j ^ 2, 0).start()
+            l_copy(j, 0, j ^ 2, 0).start()
+            for h in range(HALVES):
                 l_copy(j, h, j ^ 1, 1).start()
 
     first, rest = range(PIECES // 2), range(PIECES // 2, PIECES)
@@ -124,21 +124,25 @@
         for j in range(sections - 1):
             @pl.when((p > j) & (c == j))
             def _():
-                for h in range(HALVES):
-                    l_copy(j, h, j ^ 2, 0).wait_send()
+                l_copy(j, HALVES - 1, j ^ 2, 0).wait_send()
         each_piece(lambda m: swap(m).start())
 
     dinv_copy.wait()
     d_hi[...], d_lo[...] = split(dinv[...])
     fac_copy.wait()
-    pl.when((p == last) & (pair == 1))(swap_late)
 
     for j in range(sections - 1):
         @pl.when((p > j) & in_head & (c == j))
         def _():
             l_hi[j], l_lo[j] = split(fac[:block])
-
-        @pl.when((p > j) & in_head & (c == (j ^ 2)))
+            for h in range(1, HALVES):
+                l_copy(j, h - 1, j ^ 2, 0).wait_send()
+                l_copy(j, h, j ^ 2, 0).start()
+
+    pl.when((p == last) & (pair == 1))(swap_late)
+
+    for j in range(sections - 1):
+        @pl.when((p > j) & in_head & folded & (c == (j ^ 2)))
         def _():
             for h in range(HALVES):
                 l_forward(j, h).wait_recv()
@@ -146,7 +150,7 @@
             l_hi[j], l_lo[j] = split(l_in[j])
 
     for j in range(sections - 1):
-        @pl.when((p > j) & in_head & ((c == (j ^ 1)) | (c == (j ^ 3))))
+        @pl.when((p > j) & in_head & folded & ((c == (j ^ 1)) | (c == (j ^ 3))))
         def _():
             for h in range(HALVES):
                 l_forward(j, h).wait_recv()
@@ -198,12 +202,34 @@
                 m_hi[...], m_lo[...] = split(chain)
 
         for j in range(sections - 1):
-            @pl.when((p > j + 1) | ((p == j + 1) & jnp.logical_not(folded)))
+            @pl.when((p > j + 1) & folded)
             def _():
                 for s in range(SUBS):
                     head_copy(s, last, j).wait_recv()
                     publish(x_head.at[j], j, s, start)
                 acc[...] -= contract(x_head[j], l_hi[j], l_lo[j])
+
+        @pl.when(jnp.logical_not(folded))
+        def _():
+            for h in range(HALVES):
+                rows = pl.ds(h * half, half)
+                for j in range(sections - 2):
+                    @pl.when((p > j) & (c == (j ^ 2)))
+                    def _():
+                        l_forward(j, h).wait_recv()
+                        l_forward(j, h).start()
+                for j in range(sections - 2):
+                    @pl.when((p > j) & (c == (j ^ 3)))
+                    def _():
+                        l_forward(j, h).wait_recv()
+
+                    @pl.when(p > j)
+                    def _():
+                        if h == 0:
+                            for s in range(SUBS):
+                                head_copy(s, last, j).wait_recv()
+                                publish(x_head.at[j], j, s, start)
+                        acc[:, rows] -= contract(x_head[j], *split(l_in[j, rows]))
 
         acc[...] = contract(acc[...], d_hi[...], d_lo[...])
         for s in range(SUBS):
@@ -396,8 +422,8 @@
         out_shape=jax.ShapeDtypeStruct(right_side.shape, f32),
         in_specs=[
             pl.BlockSpec(memory_space=pltpu.VMEM),
-            pl.BlockSpec(memory_space=pl.ANY),
-            pl.BlockSpec(memory_space=pl.ANY),
+            pl.BlockSpec(memory_space=pltpu.HBM),
+            pl.BlockSpec(memory_space=pltpu.HBM),
         ],
         out_specs=pl.BlockSpec(memory_space=pltpu.VMEM),
         scratch_shapes=[
@@ -416,7 +442,7 @@
             dma((2, 2, 2, SUBS)), dma((2, 2, SUBS)), dma((PIECES,)), dma((PIECES,)),
         ],
         compiler_params=pltpu.CompilerParams(
-            collective_id=0, has_side_effects=True, vmem_limit_bytes=60 * 1024 * 1024
+            collective_id=0, has_side_effects=True, vmem_limit_bytes=40 * 1024 * 1024
         ),
         name="solve_window",
     )(right_side, factor, inverses)

time: 60.5 us -> 66.2 us (1.094)
  local copies, waits for them, and re-layouts: 1.89 us -> 5.61 us
  Pallas kernels: 58.4 us -> 60.3 us
    unnamed x1 -> x7, local copies, waits for them, and re-layouts: 1.89 us -> 5.61 us
    pallas_call x1, Pallas kernels: 58.4 us -> 60.3 us  [per_device(): pl.pallas_call(functools.partial(kernel, n_prow, sections), out_shape=jax...]
where the time goes in v7:
time: 66.2 us; the launch traced here: 66 us
  Pallas kernels  60.3 us (91%)
  local copies, waits for them, and re-layouts  5.61 us (8%)
    pallas_call x1, Pallas kernels, per_device(): pl.pallas_call(functools.partial(kernel, n_prow, sections), out_shape=jax...  60.3 us
    unnamed x7, local copies, waits for them, and re-layouts  5.61 us

profile of v7, /device:TPU:29, one launch (start us, length us, event | category | flops | bytes accessed | tf_op | source)
XLA Modules:
  0.0 66.0 jit_solution(10307257780452592698)
XLA Ops:
  0.0 0.0 copy-start
  0.0 2.2 %copy-done = f32[2048,512]{1,0:T(8,128)S(1)} copy-done((f32[2048,512]{1,0:T(8,128)S(1)}, f32[2048,512]{1,0:T(8,128)}, u32[]{:S(2)}) %copy-start) | copy-done | bytes 4194328
  2.2 0.0 copy-start.1
  2.2 1.6 %copy-done.1 = f32[1024,512]{1,0:T(8,128)S(1)} copy-done((f32[1024,512]{1,0:T(8,128)S(1)}, f32[1024,512]{1,0:T(8,128)}, u32[]{:S(2)}) %copy-start.1) | copy-done | bytes 2097176
  3.8 0.0 copy-start.2
  3.8 1.0 %copy-done.2 = f32[128,1024]{1,0:T(8,128)S(1)} copy-done((f32[128,1024]{1,0:T(8,128)S(1)}, f32[128,1024]{1,0:T(8,128)}, u32[]{:S(2)}) %copy-start.2) | copy-done | bytes 524312
  4.8 60.3 %solve_window.1 = f32[128,1024]{1,0:T(8,128)S(1)} custom-call(f32[128,1024]{1,0:T(8,128)S(1)} %copy-done.2, f32[1024,512]{1,0:T(8,128)S(1)} %copy-done.1, f32[2048,512]{1,0:T(8,128)S(1)} %copy-done), custom_call_target="tpu_custom_call" | custom-call | tf_op jit(solution)/shard_map/solve_window/pallas_call | solution.py:420
  65.2 0.8 %copy.5 = f32[128,1024]{1,0:T(8,128)} copy(f32[128,1024]{1,0:T(8,128)S(1)} %solve_window.1) | data formatting | bytes 1048576
Async XLA Ops:
  0.0 2.2 %copy-start = (f32[2048,512]{1,0:T(8,128)S(1)}, f32[2048,512]{1,0:T(8,128)}, u32[]{:S(2)}) copy-start(f32[2048,512]{1,0:T(8,128)} %inverses.1) | copy-start | bytes 12582916
  2.2 1.6 %copy-start.1 = (f32[1024,512]{1,0:T(8,128)S(1)}, f32[1024,512]{1,0:T(8,128)}, u32[]{:S(2)}) copy-start(f32[1024,512]{1,0:T(8,128)} %factor.1) | copy-start | bytes 6291460
  3.8 1.0 %copy-start.2 = (f32[128,1024]{1,0:T(8,128)S(1)}, f32[128,1024]{1,0:T(8,128)}, u32[]{:S(2)}) copy-start(f32[128,1024]{1,0:T(8,128)} %rhs.1) | copy-start | bytes 1572868

commit v8 on v6

--- a/solution.py
+++ b/solution.py
@@ -8,7 +8,7 @@
 from jax.sharding import PartitionSpec as P
 
 MESH = pl.DeviceIdType.MESH
-SUBS = 2
+SUBS = 4
 HALVES = 2
 PIECES = 4
 

time: 60.5 us -> 59.5 us (0.983); the launches traced: 60.3 us -> 58.7 us
  Pallas kernels: 58.4 us -> 56.8 us
    pallas_call x1, Pallas kernels: 58.4 us -> 56.8 us  [per_device(): pl.pallas_call(functools.partial(kernel, n_prow, sections), out_shape=jax...]
where the time goes in v8:
time: 59.5 us; the launch traced here: 58.7 us
  Pallas kernels  56.8 us (95%)
  local copies, waits for them, and re-layouts  1.89 us (3%)
    pallas_call x1, Pallas kernels, per_device(): pl.pallas_call(functools.partial(kernel, n_prow, sections), out_shape=jax...  56.8 us
    unnamed x1, local copies, waits for them, and re-layouts  1.89 us

profile of v8, /device:TPU:29, one launch (start us, length us, event | category | flops | bytes accessed | tf_op | source)
XLA Modules:
  0.0 58.7 jit_solution(17387900509130530658)
XLA Ops:
  0.0 56.8 %solve_window.1 = f32[128,1024]{1,0:T(8,128)} custom-call(f32[128,1024]{1,0:T(8,128)} %rhs.1, f32[1024,512]{1,0:T(8,128)} %factor.1, f32[2048,512]{1,0:T(8,128)} %inverses.1), custom_call_target="tpu_custom_call" | custom-call | tf_op jit(solution)/shard_map/solve_window/pallas_call | solution.py:394
  56.8 1.9 %copy.5 = f32[128,1024]{1,0:T(8,128)} copy(f32[128,1024]{1,0:T(8,128)} %solve_window.1) | data formatting | bytes 1048576
